TPU v7x, 512 devices: a whole 4x4x16 slice. The times are simulated.
512 devices in a mesh: pulse: 64 (over z, x), range: 8 (over y, core).
Axes of the slice: x: 4, y: 4, z: 16, core: 2. Of those that a mesh axis runs over, the one named last changes fastest.
Arguments:
- echo: bfloat16 [128, 2, 32768], P('pulse', None, 'range'), may hold values from -6 to 6
- chirp_phase: float32 [256], replicated, may hold values from -0.5 to 201.5624
- rec_phase: float32 [8, 8192, 2], P('range', 'pulse'), may hold values from -3.140625 to 3.140625
- rec_start: int32 [8, 8192], P('range', 'pulse'), may hold values from 0 to 32256
- rec_owner: int32 [8, 8192, 1], P('range', 'pulse'), may hold values from 0 to 511; in each aligned block of 128 rows (0 to 127, 128 to 255, ..., all dimensions but the last counted through in order) at most 2 rows name the same one
- rec_row: int32 [8, 8192], P('range', 'pulse'), may hold values from 0 to 63
- rec_weight: float32 [8, 8192], P('range', 'pulse'), may hold values from 0.2 to 1
- rec_count: int32 [8, 64], P('range', 'pulse'), may hold values from 96 to 128, as said below
- prior: bfloat16 [2048, 2, 4096], P('pulse', None, 'range'), may hold values from -6 to 6
- interp_weight: bfloat16 [64, 32], replicated, may hold values from -1 to 1
Outputs:
- tiles: float32 [4096, 2, 4096], P('pulse', None, 'range')
Inputs may be any that keep to these rules, and one draw needn't show every extreme that they name: `rec_owner`: in each aligned block of 128 record slots (one device's slots) no owner is named more than 2 times. Owner o is the tile of pulse index o // 8 and range index o % 8, 8 being the number of range devices. `rec_count`: some subimage has all 128 slots live.
All inputs are finite; a program needn't handle non-finite values.
Results may differ from a plain program's by a relative error of at most 0.0034.
Values may be sent and summed in bfloat16 or wider, within the bound.
A program may use at most 64 MiB of HBM per device.

v0:
```python
import jax
import jax.numpy as jnp
from jax import lax
from jax.sharding import PartitionSpec as P

SEG = 512


def shifted(block, axis, distance):
    devices = range(lax.axis_size(axis))
    route = [(i - distance, i) for i in devices if i - distance in devices]
    return lax.ppermute(block, axis, route)


def chirp_matrix(chirp_phase):
    tap_count = chirp_phase.shape[0]
    tap_scale = 1.0 / jnp.sqrt(jnp.float32(tap_count))
    real_taps = jnp.cos(chirp_phase) * tap_scale
    imag_taps = jnp.sin(chirp_phase) * tap_scale

    def banded(values):
        padded = jnp.concatenate([values, jnp.zeros((tap_count + 1,), jnp.float32)])
        return (
            jnp.tile(padded, tap_count)[: 2 * tap_count * tap_count]
            .reshape(tap_count, 2 * tap_count)
            .T
        )

    real_band = banded(real_taps)
    imag_band = banded(imag_taps)
    upper = jnp.concatenate([real_band, -imag_band], axis=1)
    lower = jnp.concatenate([imag_band, real_band], axis=1)
    return jnp.concatenate([upper, lower], axis=0).astype(jnp.bfloat16)


def compress(echo_block, tail_rim, filter_matrix):
    pulses, planes, bin_count = echo_block.shape
    tap_count = filter_matrix.shape[1] // 2
    block_count = bin_count // tap_count
    extended = jnp.concatenate([echo_block, tail_rim], axis=2)
    left_half = extended[:, :, :bin_count].reshape(pulses, planes, block_count, tap_count)
    right_half = extended[:, :, tap_count:].reshape(pulses, planes, block_count, tap_count)
    windows = jnp.concatenate([left_half, right_half], axis=3)
    windows = windows.transpose(0, 2, 1, 3).reshape(pulses * block_count, 2 * planes * tap_count)
    filtered = jnp.dot(windows, filter_matrix, preferred_element_type=jnp.float32)
    filtered = filtered.reshape(pulses, block_count, planes, tap_count).transpose(0, 2, 1, 3)
    return filtered.reshape(pulses, planes, bin_count).astype(jnp.bfloat16)


def cut_windows(block_table, starts):
    block_total = block_table.shape[0]
    first_block = starts // SEG
    second_block = jnp.minimum(first_block + 1, block_total - 1)
    offsets = starts % SEG
    paired = jnp.concatenate([block_table[first_block], block_table[second_block]], axis=3)
    for bit_number in range((SEG - 1).bit_length()):
        step_size = 1 << bit_number
        moved = jnp.concatenate(
            [paired[..., step_size:], jnp.zeros(paired.shape[:-1] + (step_size,), paired.dtype)],
            axis=3,
        )
        chosen = (offsets // step_size % 2 == 1)[:, None, None, None]
        paired = jnp.where(chosen, moved, paired)
    return paired[..., :SEG]


def form_records(block_table, starts, phases, scales):
    windows = cut_windows(block_table, starts)
    cosine = jnp.cos(phases).astype(jnp.bfloat16)
    sine_part = jnp.sin(phases).astype(jnp.bfloat16)
    real_part = windows[:, :, 0]
    imag_part = windows[:, :, 1]
    out_real = jnp.einsum(
        "bk,bks->bs", cosine, real_part, preferred_element_type=jnp.float32
    ) - jnp.einsum("bk,bks->bs", sine_part, imag_part, preferred_element_type=jnp.float32)
    out_imag = jnp.einsum(
        "bk,bks->bs", cosine, imag_part, preferred_element_type=jnp.float32
    ) + jnp.einsum("bk,bks->bs", sine_part, real_part, preferred_element_type=jnp.float32)
    return (jnp.stack([out_real, out_imag], axis=1) * scales[:, None, None]).astype(jnp.bfloat16)


def on_device(
    echo,
    chirp_phase,
    rec_phase,
    rec_start,
    rec_owner,
    rec_row,
    rec_weight,
    rec_count,
    prior,
    interp_weight,
):
    filter_matrix = chirp_matrix(chirp_phase)
    tap_count = chirp_phase.shape[0]
    tail_rim = shifted(echo[:, :, :tap_count], "range", -1)
    profiles = lax.all_gather(compress(echo, tail_rim, filter_matrix), "range", axis=2, tiled=True)
    pulses, planes, bin_total = profiles.shape
    block_table = profiles.reshape(pulses, planes, bin_total // SEG, SEG).transpose(2, 0, 1, 3)
    slot_count = rec_start.shape[1]
    starts = rec_start[0]
    phases = rec_phase[0]
    owners = rec_owner[0, :, 0]
    dest_rows = rec_row[0]
    weights = rec_weight[0]
    live_mask = (jnp.arange(slot_count) < rec_count[0, 0]).astype(jnp.float32)
    scales = live_mask * weights / jnp.sqrt(jnp.float32(pulses))
    block_size = min(64, slot_count)
    group_count = slot_count // block_size

    def form_group(items):
        return form_records(block_table, items[0], items[1], items[2])

    records = lax.map(
        form_group,
        (
            starts.reshape(group_count, block_size),
            phases.reshape(group_count, block_size, pulses),
            scales.reshape(group_count, block_size),
        ),
    )
    records = records.reshape(slot_count, 2 * SEG)
    pulse_count = lax.axis_size("pulse")
    range_count = lax.axis_size("range")
    owner_total = pulse_count * range_count
    capacity = max(2, 3 * slot_count // (2 * owner_total))
    owner_marks = (owners[:, None] == jnp.arange(owner_total)[None, :]).astype(jnp.int32)
    earlier = jnp.cumsum(owner_marks, axis=0) - owner_marks
    slot_rank = jnp.sum(earlier * owner_marks, axis=1)
    slot_index = owners * capacity + slot_rank
    placement = slot_index[None, :] == jnp.arange(owner_total * capacity)[:, None]
    outgoing = jnp.dot(
        placement.astype(jnp.bfloat16), records, preferred_element_type=jnp.float32
    ).astype(jnp.bfloat16)
    row_slots = jnp.sum(placement.astype(jnp.int32) * dest_rows[None, :], axis=1)
    outgoing = outgoing.reshape(pulse_count, range_count, capacity, 2, SEG)
    row_slots = row_slots.reshape(pulse_count, range_count, capacity)
    incoming, incoming_rows = (
        lax.all_to_all(
            lax.all_to_all(outgoing, "pulse", split_axis=0, concat_axis=0, tiled=True),
            "range",
            split_axis=1,
            concat_axis=1,
            tiled=True,
        ),
        lax.all_to_all(
            lax.all_to_all(row_slots, "pulse", split_axis=0, concat_axis=0, tiled=True),
            "range",
            split_axis=1,
            concat_axis=1,
            tiled=True,
        ),
    )
    incoming = incoming.reshape(-1, 2, SEG)
    incoming_rows = incoming_rows.reshape(-1)
    out_rows = interp_weight.shape[0]
    tile_image = jnp.einsum("rm,mcs->rcs", interp_weight, prior, preferred_element_type=jnp.float32)
    row_table = (incoming_rows[:, None] == jnp.arange(out_rows)[None, :]).astype(jnp.bfloat16)
    tile_image = tile_image + jnp.einsum(
        "jr,jcs->rcs", row_table, incoming, preferred_element_type=jnp.float32
    )
    return tile_image


def solution(mesh):
    placed = (
        P("pulse", None, "range"),
        P(),
        P("range", "pulse", None),
        P("range", "pulse"),
        P("range", "pulse", None),
        P("range", "pulse"),
        P("range", "pulse"),
        P("range", "pulse"),
        P("pulse", None, "range"),
        P(),
    )
    return jax.shard_map(
        on_device, mesh=mesh, in_specs=placed, out_specs=P("pulse", None, "range"), check_vma=False
    )
```

profile of v0, /device:TPU:1, one launch (start us, length us, event | category | flops | bytes accessed | tf_op | source)
XLA Modules:
  0.0 257.0 jit_solution(12730651310429651620)
XLA Ops:
  0.7 8.8 %collective-permute-start = (bf16[2,2,256]{2,1,0:T(2,128)(2,1)S(1)}, bf16[2,2,256]{2,1,0:T(2,128)(2,1)S(1)}, u32[]{:S(2)}, u32[]{:S(2)}) collective-permute-start(bf16[2,2,256]{2,1,0:T(2,128)(2,1)S(1)} %slice.92), channel_id=1, source_target_pairs={{1,0},{2,1},{3,2},{4,3},{5,4},{6,5},{7,6},{9,8},{10,9},{11,10},{12... | collective-permute-start | bytes 6152 | tf_op jit(solution)/shard_map/ppermute | solution.py:12
  13.1 1.1 copy.61
  14.2 12.9 %all-to-all-start = ((s32[64,8,2]{1,2,0:T(2,128)}), s32[64,8,2]{1,2,0:T(2,128)S(1)}, u32[]{:S(2)}, u32[]{:S(2)}) async-start(s32[64,8,2]{1,2,0:T(2,128)} %copy.61), calls=%async_computation | async-start | bytes 131072 | tf_op jit(solution)/shard_map/all_to_all | solution.py:147
  33.8 13.5 %all_gather.3 = bf16[2,2,32768]{2,1,0:T(2,128)(2,1)S(1)} all-gather(bf16[2,2,4096]{2,1,0:T(2,128)(2,1)S(1)} %convert_element_type.57), channel_id=1, replica_groups=mesh['pulse'=64,'range'=8] {'range'}, dimensions={2}, use_global_device_ids=true | all-gather | bytes 294912 | tf_op jit(solution)/shard_map/all_gather | solution.py:97
  47.8 42.9 %while.13 = (s32[]{:T(128)}, bf16[2,64,2,512]{3,2,1,0:T(2,128)(2,1)S(1)}, f32[2,64,2]{1,0,2:T(2,128)S(1)}, s32[2,64]{1,0:T(2,128)S(1)}, bf16[64,2,2,512]{3,2,1,0...) while((s32[]{:T(128)}, bf16[2,64,2,512]{3,2,1,0:T(2,128)(2,1)S(1)}, f32[2,64,2]{1,0,2:T(2,128)S(1)}, ...), condition=%wide.region_4.5_spmd, body=%wide.region_3.4_spmd.sunk | while | flops 3162434 | bytes 28723936 | solution.py:114
  48.0 1.1 gather_fusion
  49.3 1.1 gather_fusion.1
  50.6 1.0 slice.137
  52.7 1.0 slice.138
  54.7 1.0 slice.139
  56.7 1.0 slice.140
  58.7 1.0 slice.141
  60.7 1.0 slice.142
  62.7 1.0 slice.143
  69.3 1.1 gather_fusion
  70.5 1.1 gather_fusion.1
  73.9 1.0 slice.138
  75.9 1.0 slice.139
  77.9 1.0 slice.140
  79.9 1.0 slice.141
  81.9 1.0 slice.142
  83.9 1.0 slice.143
  91.4 2.7 %reshape.460 = bf16[64,8,2,2,512]{4,3,2,1,0:T(2,128)(2,1)} reshape(bf16[1024,1024]{1,0:T(8,128)(2,1)S(1)} %convolution_convert_fusion) | data formatting | bytes 4194304 | tf_op jit(solution)/shard_map/reshape | solution.py:136
  94.1 14.8 %all-to-all-start.2 = ((bf16[64,8,2,2,512]{4,3,2,1,0:T(2,128)(2,1)}), bf16[64,8,2,2,512]{4,3,2,1,0:T(2,128)(2,1)S(1)}, u32[]{:S(2)}, u32[]{:S(2)}) async-start(bf16[64,8,2,2,512]{4,3,2,1,0:T(2,128)(2,1)} %reshape.460), calls=%async_computation.2 | async-start | bytes 4194304 | tf_op jit(solution)/shard_map/all_to_all | solution.py:140
  109.7 96.3 %all-to-all-done.2 = bf16[64,8,2,2,512]{4,3,2,1,0:T(2,128)(2,1)S(1)} async-done(((bf16[64,8,2,2,512]{4,3,2,1,0:T(2,128)(2,1)}), bf16[64,8,2,2,512]{4,3,2,1,0:T(2,128)(2,1)S(1)}, u32[]{:S(2)}, u32[]{:S(2)}) %all-to-all-start.2) | async-done | bytes 2097184 | tf_op jit(solution)/shard_map/all_to_all | solution.py:140
  206.0 8.1 %all-to-all-start.1 = ((s32[8,1,128]{2,1,0:T(1,128)}), s32[8,1,128]{2,1,0:T(1,128)S(1)}, u32[]{:S(2)}, u32[]{:S(2)}) async-start(s32[8,1,128]{2,1,0:T(1,128)} %reshape.511), calls=%async_computation.1 | async-start | bytes 8192 | tf_op jit(solution)/shard_map/all_to_all | solution.py:146
  214.1 3.0 %copy.68 = bf16[64,8,2,2,512]{4,3,2,0,1:T(2,128)(2,1)} copy(bf16[64,8,2,2,512]{4,3,2,1,0:T(2,128)(2,1)S(1)} %all-to-all-done.2) | data formatting | bytes 4194304 | tf_op jit(solution)/shard_map/all_to_all | solution.py:140
  217.0 1.5 all-to-all-done.1
  218.6 4.2 %all-to-all-start.3 = ((bf16[64,8,2,2,512]{4,3,2,0,1:T(2,128)(2,1)}), bf16[64,8,2,2,512]{4,3,2,0,1:T(2,128)(2,1)S(1)}, u32[]{:S(2)}, u32[]{:S(2)}) async-start(bf16[64,8,2,2,512]{4,3,2,0,1:T(2,128)(2,1)} %copy.68), calls=%async_computation.3 | async-start | bytes 4194304 | tf_op jit(solution)/shard_map/all_to_all | solution.py:139
  224.6 24.5 %all-to-all-done.3 = bf16[64,8,2,2,512]{4,3,2,0,1:T(2,128)(2,1)S(1)} async-done(((bf16[64,8,2,2,512]{4,3,2,0,1:T(2,128)(2,1)}), bf16[64,8,2,2,512]{4,3,2,0,1:T(2,128)(2,1)S(1)}, u32[]{:S(2)}, u32[]{:S(2)}) %all-to-all-start.3) | async-done | bytes 2097184 | tf_op jit(solution)/shard_map/all_to_all | solution.py:139
  249.1 3.8 %copy.69 = bf16[64,8,2,2,512]{4,2,1,0,3:T(2,128)(2,1)} copy(bf16[64,8,2,2,512]{4,3,2,0,1:T(2,128)(2,1)S(1)} %all-to-all-done.3) | data formatting | bytes 4194304 | tf_op jit(solution)/shard_map/all_to_all | solution.py:139
  252.9 2.7 %reshape.461 = bf16[1024,2,512]{2,0,1:T(8,128)(2,1)S(1)} reshape(bf16[64,8,2,2,512]{4,2,1,0,3:T(2,128)(2,1)} %copy.69) | data formatting | bytes 4194304 | tf_op jit(solution)/shard_map/reshape | solution.py:154
  (137 shorter events, 39.7 us)
Async XLA Ops:
  0.0 222.8 %copy-start = (bf16[32,2,512]{2,1,0:T(2,128)(2,1)S(1)}, bf16[32,2,512]{2,1,0:T(2,128)(2,1)}, u32[]{:S(2)}) copy-start(bf16[32,2,512]{2,1,0:T(2,128)(2,1)} %param.20) | copy-start | bytes 196612
  0.7 32.5 %collective-permute-start = (bf16[2,2,256]{2,1,0:T(2,128)(2,1)S(1)}, bf16[2,2,256]{2,1,0:T(2,128)(2,1)S(1)}, u32[]{:S(2)}, u32[]{:S(2)}) collective-permute-start(bf16[2,2,256]{2,1,0:T(2,128)(2,1)S(1)} %slice.92), channel_id=1, source_target_pairs={{1,0},{2,1},{3,2},{4,3},{5,4},{6,5},{7,6},{9,8},{10,9},{11,10},{12... | collective-permute-start | bytes 6152 | tf_op jit(solution)/shard_map/ppermute | solution.py:12
  10.5 18.0 %copy-start.4 = (f32[256]{0:T(256)S(1)}, f32[256]{0:T(256)}, u32[]{:S(2)}) copy-start(f32[256]{0:T(256)} %param.13) | copy-start | bytes 3076
  14.2 80.0 %all-to-all-start = ((s32[64,8,2]{1,2,0:T(2,128)}), s32[64,8,2]{1,2,0:T(2,128)S(1)}, u32[]{:S(2)}, u32[]{:S(2)}) async-start(s32[64,8,2]{1,2,0:T(2,128)} %copy.61), calls=%async_computation | async-start | bytes 131072 | tf_op jit(solution)/shard_map/all_to_all | solution.py:147
  28.4 1.9 copy-start.5
  28.7 3.1 %copy-start.3 = (f32[1,128,2]{1,2,0:T(2,128)S(1)}, f32[1,128,2]{1,2,0:T(2,128)}, u32[]{:S(2)}) copy-start(f32[1,128,2]{1,2,0:T(2,128)} %param.14) | copy-start | bytes 3076
  28.7 3.7 %copy-start.6 = (s32[1,128]{1,0:T(1,128)S(1)}, s32[1,128]{1,0:T(1,128)}, u32[]{:S(2)}) copy-start(s32[1,128]{1,0:T(1,128)} %param.15) | copy-start | bytes 1540
  28.7 4.5 %copy-start.1 = (bf16[2,2,4096]{2,1,0:T(2,128)(2,1)S(1)}, bf16[2,2,4096]{2,1,0:T(2,128)(2,1)}, u32[]{:S(2)}) copy-start(bf16[2,2,4096]{2,1,0:T(2,128)(2,1)} %param.12) | copy-start | bytes 98308
  94.1 111.8 %all-to-all-start.2 = ((bf16[64,8,2,2,512]{4,3,2,1,0:T(2,128)(2,1)}), bf16[64,8,2,2,512]{4,3,2,1,0:T(2,128)(2,1)S(1)}, u32[]{:S(2)}, u32[]{:S(2)}) async-start(bf16[64,8,2,2,512]{4,3,2,1,0:T(2,128)(2,1)} %reshape.460), calls=%async_computation.2 | async-start | bytes 4194304 | tf_op jit(solution)/shard_map/all_to_all | solution.py:140
  206.0 12.6 %all-to-all-start.1 = ((s32[8,1,128]{2,1,0:T(1,128)}), s32[8,1,128]{2,1,0:T(1,128)S(1)}, u32[]{:S(2)}, u32[]{:S(2)}) async-start(s32[8,1,128]{2,1,0:T(1,128)} %reshape.511), calls=%async_computation.1 | async-start | bytes 8192 | tf_op jit(solution)/shard_map/all_to_all | solution.py:146
  217.0 5.7 %copy-start.2 = (bf16[64,32]{0,1:T(8,128)(2,1)S(1)}, bf16[64,32]{0,1:T(8,128)(2,1)}, u32[]{:S(2)}) copy-start(bf16[64,32]{0,1:T(8,128)(2,1)} %param.21) | copy-start | bytes 12292
  218.6 30.6 %all-to-all-start.3 = ((bf16[64,8,2,2,512]{4,3,2,0,1:T(2,128)(2,1)}), bf16[64,8,2,2,512]{4,3,2,0,1:T(2,128)(2,1)S(1)}, u32[]{:S(2)}, u32[]{:S(2)}) async-start(bf16[64,8,2,2,512]{4,3,2,0,1:T(2,128)(2,1)} %copy.68), calls=%async_computation.3 | async-start | bytes 4194304 | tf_op jit(solution)/shard_map/all_to_all | solution.py:139
where the time goes:
time: 258 us; the launch traced here: 257 us
  waiting for transfers between devices  122 us (47%)
  starting transfers between devices  48.8 us (19%)
  local copies, waits for them, and re-layouts  42.8 us (17%)
  other arithmetic  23.8 us (9%)
  blocking collectives  13.5 us (5%)
  matrix products  3.96 us (2%)
    all_to_all x1, waiting for transfers between devices, on_device(): lax.all_to_all(outgoing, 'pulse', split_axis=0, concat_axis=0, tiled=True)  96.3 us
    all_to_all x1, waiting for transfers between devices, on_device(): lax.all_to_all(lax.all_to_all(outgoing, 'pulse', split_axis=0, concat_axi...  24.5 us
    select_n x18, other arithmetic, cut_windows(): paired = jnp.where(chosen, moved, paired)  16.4 us
    slice x18, local copies, waits for them, and re-layouts, cut_windows(): paired[..., step_size:]  15.4 us
    all_to_all x1, starting transfers between devices, on_device(): lax.all_to_all(outgoing, 'pulse', split_axis=0, concat_axis=0, tiled=True)  14.8 us
    all_gather x1, blocking collectives, on_device(): lax.all_gather(compress(echo, tail_rim, filter_matrix), 'range', axis=2,...  13.5 us
    all_to_all x1, starting transfers between devices, on_device(): lax.all_to_all(row_slots, 'pulse', split_axis=0, concat_axis=0, tiled=True)  12.9 us
    ppermute x1, starting transfers between devices, shifted(): return lax.ppermute(block, axis, route)  8.77 us
  transfers between devices with their start and end apart: 5, of which 3 were waited for; matrix products, arithmetic and copies ran while one was open for 24% of the time, Pallas kernels for 0%

commit v1 on v0

--- a/solution.py
+++ b/solution.py
@@ -94,7 +94,15 @@
     filter_matrix = chirp_matrix(chirp_phase)
     tap_count = chirp_phase.shape[0]
     tail_rim = shifted(echo[:, :, :tap_count], "range", -1)
-    profiles = lax.all_gather(compress(echo, tail_rim, filter_matrix), "range", axis=2, tiled=True)
+    profiles = jnp.concatenate(
+        lax.all_to_all(
+            jnp.stack([compress(echo, tail_rim, filter_matrix)] * lax.axis_size("range")),
+            "range",
+            0,
+            0,
+        ),
+        axis=2,
+    )
     pulses, planes, bin_total = profiles.shape
     block_table = profiles.reshape(pulses, planes, bin_total // SEG, SEG).transpose(2, 0, 1, 3)
     slot_count = rec_start.shape[1]

time: 258 us -> 248 us (0.961)
  blocking collectives: 13.5 us -> 0 us
  starting transfers between devices: 48.8 us -> 56.3 us
  other arithmetic: 23.8 us -> 21.2 us
    all_gather x1 -> x0, blocking collectives: 13.5 us -> none  [on_device(): lax.all_gather(compress(echo, tail_rim, filter_matrix), 'range', axis=2,...]
    all_to_all x0 -> x1, starting transfers between devices: none -> 3.36 us  [on_device(): lax.all_to_all(jnp.stack([compress(echo, tail_rim, filter_matrix)] * lax....]
    all_to_all x1, waiting for transfers between devices: 96.3 us -> 93 us  [on_device(): lax.all_to_all(outgoing, 'pulse', split_axis=0, concat_axis=0, tiled=True)]
    all_to_all x1, starting transfers between devices: 8.09 us -> 10.7 us  [on_device(): lax.all_to_all(lax.all_to_all(row_slots, 'pulse', split_axis=0, concat_ax...]
  transfers between devices with their start and end apart: 5 -> 6, of which waited for: 3 -> 4; matrix products, arithmetic and copies ran while one was open for 24% -> 24% of each run, Pallas kernels for 0% -> 0%
where the time goes in v1:
time: 248 us; the launch traced here: 247 us
  waiting for transfers between devices  120 us (48%)
  starting transfers between devices  56.3 us (23%)
  local copies, waits for them, and re-layouts  43.9 us (18%)
  other arithmetic  21.2 us (9%)
  matrix products  3.97 us (2%)
    all_to_all x1, waiting for transfers between devices, on_device(): lax.all_to_all(outgoing, 'pulse', split_axis=0, concat_axis=0, tiled=True)  93 us
    all_to_all x1, waiting for transfers between devices, on_device(): lax.all_to_all(lax.all_to_all(outgoing, 'pulse', split_axis=0, concat_axi...  24.5 us
    select_n x18, other arithmetic, cut_windows(): paired = jnp.where(chosen, moved, paired)  16.4 us
    slice x18, local copies, waits for them, and re-layouts, cut_windows(): paired[..., step_size:]  15.4 us
    all_to_all x1, starting transfers between devices, on_device(): lax.all_to_all(row_slots, 'pulse', split_axis=0, concat_axis=0, tiled=True)  14.8 us
    all_to_all x1, starting transfers between devices, on_device(): lax.all_to_all(outgoing, 'pulse', split_axis=0, concat_axis=0, tiled=True)  14.5 us
    all_to_all x1, starting transfers between devices, on_device(): lax.all_to_all(lax.all_to_all(row_slots, 'pulse', split_axis=0, concat_ax...  10.7 us
    ppermute x1, starting transfers between devices, shifted(): return lax.ppermute(block, axis, route)  8.77 us
  transfers between devices with their start and end apart: 6, of which 4 were waited for; matrix products, arithmetic and copies ran while one was open for 24% of the time, Pallas kernels for 0%

profile of v1, /device:TPU:1, one launch (start us, length us, event | category | flops | bytes accessed | tf_op | source)
XLA Modules:
  0.0 247.3 jit_solution(6578514160226730536)
XLA Ops:
  0.7 8.8 %collective-permute-start = (bf16[2,2,256]{2,1,0:T(2,128)(2,1)S(1)}, bf16[2,2,256]{2,1,0:T(2,128)(2,1)S(1)}, u32[]{:S(2)}, u32[]{:S(2)}) collective-permute-start(bf16[2,2,256]{2,1,0:T(2,128)(2,1)S(1)} %slice.92), channel_id=1, source_target_pairs={{1,0},{2,1},{3,2},{4,3},{5,4},{6,5},{7,6},{9,8},{10,9},{11,10},{12... | collective-permute-start | bytes 6152 | tf_op jit(solution)/shard_map/ppermute | solution.py:12
  14.4 3.4 %all-to-all-start.2 = ((bf16[8,2,2,4096]{3,2,1,0:T(2,128)(2,1)}), bf16[8,2,2,4096]{3,2,1,0:T(2,128)(2,1)S(1)}, u32[]{:S(2)}, u32[]{:S(2)}) async-start(bf16[8,2,2,4096]{3,2,1,0:T(2,128)(2,1)} %stack.8), calls=%async_computation.2 | async-start | bytes 524288 | tf_op jit(solution)/shard_map/all_to_all | solution.py:98
  21.6 1.1 copy.63
  22.6 1.0 all-to-all-done.2
  23.6 14.8 %all-to-all-start = ((s32[64,8,2]{1,2,0:T(2,128)}), s32[64,8,2]{1,2,0:T(2,128)S(1)}, u32[]{:S(2)}, u32[]{:S(2)}) async-start(s32[64,8,2]{1,2,0:T(2,128)} %copy.63), calls=%async_computation | async-start | bytes 131072 | tf_op jit(solution)/shard_map/all_to_all | solution.py:155
  39.0 42.9 %while.13 = (s32[]{:T(128)}, bf16[2,64,2,512]{3,2,1,0:T(2,128)(2,1)S(1)}, f32[2,64,2]{1,0,2:T(2,128)S(1)}, s32[2,64]{1,0:T(2,128)S(1)}, bf16[64,2,2,512]{3,2,1,0...) while((s32[]{:T(128)}, bf16[2,64,2,512]{3,2,1,0:T(2,128)(2,1)S(1)}, f32[2,64,2]{1,0,2:T(2,128)S(1)}, ...), condition=%wide.region_4.5_spmd, body=%wide.region_3.4_spmd.sunk | while | flops 3162434 | bytes 28723936 | solution.py:122
  39.2 1.1 gather_fusion
  40.5 1.1 gather_fusion.1
  43.9 1.0 slice.138
  45.9 1.0 slice.139
  47.9 1.0 slice.140
  49.9 1.0 slice.141
  51.9 1.0 slice.142
  53.9 1.0 slice.143
  60.5 1.1 gather_fusion
  61.8 1.1 gather_fusion.1
  65.1 1.0 slice.138
  67.1 1.0 slice.139
  69.1 1.0 slice.140
  71.1 1.0 slice.141
  73.1 1.0 slice.142
  75.1 1.0 slice.143
  82.6 2.8 %reshape.463 = bf16[64,8,2,2,512]{4,3,2,1,0:T(2,128)(2,1)} reshape(bf16[1024,1024]{1,0:T(8,128)(2,1)S(1)} %convolution_convert_fusion) | data formatting | bytes 4194304 | tf_op jit(solution)/shard_map/reshape | solution.py:144
  85.4 14.5 %all-to-all-start.3 = ((bf16[64,8,2,2,512]{4,3,2,1,0:T(2,128)(2,1)}), bf16[64,8,2,2,512]{4,3,2,1,0:T(2,128)(2,1)S(1)}, u32[]{:S(2)}, u32[]{:S(2)}) async-start(bf16[64,8,2,2,512]{4,3,2,1,0:T(2,128)(2,1)} %reshape.463), calls=%async_computation.3 | async-start | bytes 4194304 | tf_op jit(solution)/shard_map/all_to_all | solution.py:148
  100.7 93.0 %all-to-all-done.3 = bf16[64,8,2,2,512]{4,3,2,1,0:T(2,128)(2,1)S(1)} async-done(((bf16[64,8,2,2,512]{4,3,2,1,0:T(2,128)(2,1)}), bf16[64,8,2,2,512]{4,3,2,1,0:T(2,128)(2,1)S(1)}, u32[]{:S(2)}, u32[]{:S(2)}) %all-to-all-start.3) | async-done | bytes 2097184 | tf_op jit(solution)/shard_map/all_to_all | solution.py:148
  193.6 10.7 %all-to-all-start.1 = ((s32[8,1,128]{2,1,0:T(1,128)}), s32[8,1,128]{2,1,0:T(1,128)S(1)}, u32[]{:S(2)}, u32[]{:S(2)}) async-start(s32[8,1,128]{2,1,0:T(1,128)} %reshape.514), calls=%async_computation.1 | async-start | bytes 8192 | tf_op jit(solution)/shard_map/all_to_all | solution.py:154
  204.3 3.0 %copy.71 = bf16[64,8,2,2,512]{4,3,2,0,1:T(2,128)(2,1)} copy(bf16[64,8,2,2,512]{4,3,2,1,0:T(2,128)(2,1)S(1)} %all-to-all-done.3) | data formatting | bytes 4194304 | tf_op jit(solution)/shard_map/all_to_all | solution.py:148
  207.3 1.6 all-to-all-done.1
  208.8 4.2 %all-to-all-start.4 = ((bf16[64,8,2,2,512]{4,3,2,0,1:T(2,128)(2,1)}), bf16[64,8,2,2,512]{4,3,2,0,1:T(2,128)(2,1)S(1)}, u32[]{:S(2)}, u32[]{:S(2)}) async-start(bf16[64,8,2,2,512]{4,3,2,0,1:T(2,128)(2,1)} %copy.71), calls=%async_computation.4 | async-start | bytes 4194304 | tf_op jit(solution)/shard_map/all_to_all | solution.py:147
  214.9 24.5 %all-to-all-done.4 = bf16[64,8,2,2,512]{4,3,2,0,1:T(2,128)(2,1)S(1)} async-done(((bf16[64,8,2,2,512]{4,3,2,0,1:T(2,128)(2,1)}), bf16[64,8,2,2,512]{4,3,2,0,1:T(2,128)(2,1)S(1)}, u32[]{:S(2)}, u32[]{:S(2)}) %all-to-all-start.4) | async-done | bytes 2097184 | tf_op jit(solution)/shard_map/all_to_all | solution.py:147
  239.4 3.8 %copy.72 = bf16[64,8,2,2,512]{4,2,1,0,3:T(2,128)(2,1)} copy(bf16[64,8,2,2,512]{4,3,2,0,1:T(2,128)(2,1)S(1)} %all-to-all-done.4) | data formatting | bytes 4194304 | tf_op jit(solution)/shard_map/all_to_all | solution.py:147
  243.1 2.7 %reshape.464 = bf16[1024,2,512]{2,0,1:T(8,128)(2,1)S(1)} reshape(bf16[64,8,2,2,512]{4,2,1,0,3:T(2,128)(2,1)} %copy.72) | data formatting | bytes 4194304 | tf_op jit(solution)/shard_map/reshape | solution.py:162
  (144 shorter events, 39.1 us)
Async XLA Ops:
  0.0 213.0 %copy-start = (bf16[32,2,512]{2,1,0:T(2,128)(2,1)S(1)}, bf16[32,2,512]{2,1,0:T(2,128)(2,1)}, u32[]{:S(2)}) copy-start(bf16[32,2,512]{2,1,0:T(2,128)(2,1)} %param.20) | copy-start | bytes 196612
  0.0 10.9 %copy-start.5 = (f32[256]{0:T(256)S(1)}, f32[256]{0:T(256)}, u32[]{:S(2)}) copy-start(f32[256]{0:T(256)} %param.13) | copy-start | bytes 3076
  0.0 10.9 %copy-start.3 = (s32[1,128,1]{1,2,0:T(1,128)S(1)}, s32[1,128,1]{1,2,0:T(1,128)}, u32[]{:S(2)}) copy-start(s32[1,128,1]{1,2,0:T(1,128)} %param.16) | copy-start | bytes 1540
  0.7 12.2 %collective-permute-start = (bf16[2,2,256]{2,1,0:T(2,128)(2,1)S(1)}, bf16[2,2,256]{2,1,0:T(2,128)(2,1)S(1)}, u32[]{:S(2)}, u32[]{:S(2)}) collective-permute-start(bf16[2,2,256]{2,1,0:T(2,128)(2,1)S(1)} %slice.92), channel_id=1, source_target_pairs={{1,0},{2,1},{3,2},{4,3},{5,4},{6,5},{7,6},{9,8},{10,9},{11,10},{12... | collective-permute-start | bytes 6152 | tf_op jit(solution)/shard_map/ppermute | solution.py:12
  11.7 1.2 copy-start.1
  12.7 5.1 %copy-start.6 = (s32[1,128]{1,0:T(1,128)S(1)}, s32[1,128]{1,0:T(1,128)}, u32[]{:S(2)}) copy-start(s32[1,128]{1,0:T(1,128)} %param.17) | copy-start | bytes 1540
  12.7 5.9 %copy-start.7 = (f32[1,128]{1,0:T(1,128)S(1)}, f32[1,128]{1,0:T(1,128)}, u32[]{:S(2)}) copy-start(f32[1,128]{1,0:T(1,128)} %param.18) | copy-start | bytes 1540
  12.7 7.2 %copy-start.4 = (f32[1,128,2]{1,2,0:T(2,128)S(1)}, f32[1,128,2]{1,2,0:T(2,128)}, u32[]{:S(2)}) copy-start(f32[1,128,2]{1,2,0:T(2,128)} %param.14) | copy-start | bytes 3076
  12.7 7.9 %copy-start.8 = (s32[1,128]{1,0:T(1,128)S(1)}, s32[1,128]{1,0:T(1,128)}, u32[]{:S(2)}) copy-start(s32[1,128]{1,0:T(1,128)} %param.15) | copy-start | bytes 1540
  14.4 9.2 %all-to-all-start.2 = ((bf16[8,2,2,4096]{3,2,1,0:T(2,128)(2,1)}), bf16[8,2,2,4096]{3,2,1,0:T(2,128)(2,1)S(1)}, u32[]{:S(2)}, u32[]{:S(2)}) async-start(bf16[8,2,2,4096]{3,2,1,0:T(2,128)(2,1)} %stack.8), calls=%async_computation.2 | async-start | bytes 524288 | tf_op jit(solution)/shard_map/all_to_all | solution.py:98
  23.6 61.7 %all-to-all-start = ((s32[64,8,2]{1,2,0:T(2,128)}), s32[64,8,2]{1,2,0:T(2,128)S(1)}, u32[]{:S(2)}, u32[]{:S(2)}) async-start(s32[64,8,2]{1,2,0:T(2,128)} %copy.63), calls=%async_computation | async-start | bytes 131072 | tf_op jit(solution)/shard_map/all_to_all | solution.py:155
  85.4 108.3 %all-to-all-start.3 = ((bf16[64,8,2,2,512]{4,3,2,1,0:T(2,128)(2,1)}), bf16[64,8,2,2,512]{4,3,2,1,0:T(2,128)(2,1)S(1)}, u32[]{:S(2)}, u32[]{:S(2)}) async-start(bf16[64,8,2,2,512]{4,3,2,1,0:T(2,128)(2,1)} %reshape.463), calls=%async_computation.3 | async-start | bytes 4194304 | tf_op jit(solution)/shard_map/all_to_all | solution.py:148
  193.6 15.2 %all-to-all-start.1 = ((s32[8,1,128]{2,1,0:T(1,128)}), s32[8,1,128]{2,1,0:T(1,128)S(1)}, u32[]{:S(2)}, u32[]{:S(2)}) async-start(s32[8,1,128]{2,1,0:T(1,128)} %reshape.514), calls=%async_computation.1 | async-start | bytes 8192 | tf_op jit(solution)/shard_map/all_to_all | solution.py:154
  207.3 5.8 %copy-start.2 = (bf16[64,32]{0,1:T(8,128)(2,1)S(1)}, bf16[64,32]{0,1:T(8,128)(2,1)}, u32[]{:S(2)}) copy-start(bf16[64,32]{0,1:T(8,128)(2,1)} %param.21) | copy-start | bytes 12292
  208.8 30.6 %all-to-all-start.4 = ((bf16[64,8,2,2,512]{4,3,2,0,1:T(2,128)(2,1)}), bf16[64,8,2,2,512]{4,3,2,0,1:T(2,128)(2,1)S(1)}, u32[]{:S(2)}, u32[]{:S(2)}) async-start(bf16[64,8,2,2,512]{4,3,2,0,1:T(2,128)(2,1)} %copy.71), calls=%async_computation.4 | async-start | bytes 4194304 | tf_op jit(solution)/shard_map/all_to_all | solution.py:147
